TPU v7x, 32 devices: a whole 2x2x4 slice. The times are simulated.
32 devices in a mesh: pipe: 4 (over z), ctx: 8 (over y, x, core).
Axes of the slice: x: 2, y: 2, z: 4, core: 2. Of those that a mesh axis runs over, the one named last changes fastest.
Arguments:
- query_projections: bfloat16 [4, 1024, 4096], P('pipe', 'ctx'), may hold values from -300 to 300
- key_states: bfloat16 [4, 1024, 512], P('pipe', 'ctx'), may hold values from -7 to 7
- value_projections: bfloat16 [4, 1024, 512], P('pipe', 'ctx'), may hold values from -6 to 6
- grad_incoming: bfloat16 [4, 1024, 4096], P('pipe', 'ctx'), may hold values from -6 to 6
- key_blocks: int32 [4, 16, 2], P('pipe', 'ctx'), may hold values from -1 to 15, as said below
Outputs:
- query_gradient: bfloat16 [4, 1024, 4096], P('pipe', 'ctx')
- key_gradient: bfloat16 [4, 1024, 512], P('pipe', 'ctx')
Inputs may be any that keep to these rules, and one draw needn't show every extreme that they name: `key_blocks`: entry 0 of every list is the query block itself. Each later entry is the parent of the one before (every block's parent lies 1 to 4 blocks before it), or -1 once a root was passed, and stays -1 after. No listed block lies on a device of ctx more than 2 devices before its query block's device, and in every draw some listed block lies exactly 2 devices before.
All inputs are finite; a program needn't handle non-finite values.
Results may differ from a plain program's by a relative error of at most 0.013.
Values may be sent and summed in bfloat16 or wider, within the bound.
A program may use at most 64 MiB of HBM per device.

v0:
```python
import jax
import jax.numpy as jnp
from jax import lax
from jax.sharding import PartitionSpec as P

QUERY_HEADS = 32
KEY_VALUE_HEADS = 4
HEAD_SIZE = 128
TREE_BLOCK_SIZE = 64
QUERY_GROUP = 8
BLOCKS_PER_RANK = 2
MAX_RANK_REACH = 2


def shifted(value, axis, steps):
    count = lax.axis_size(axis)
    pairs = [(source, (source + steps) % count) for source in range(count)]
    return lax.ppermute(value, axis, pairs)


def from_behind(array, axis, by):
    peers = lax.axis_size(axis)
    pairs = [(i, i + by) for i in range(peers) if 0 <= i + by < peers]
    return lax.ppermute(array, axis, pairs)


def attend_block(query_blk, key_sel, value_sel, grad_blk, entries, first_pos):
    entry_count, block_len, kv_heads, head_dim = key_sel.shape
    listed = entries >= 0
    clamped = jnp.maximum(entries, 0)
    query_pos = first_pos + jnp.arange(query_blk.shape[0], dtype=jnp.int32)
    key_pos = clamped[:, None] * block_len + jnp.arange(block_len, dtype=jnp.int32)[None, :]
    listed_keys = jnp.broadcast_to(listed[:, None], (entry_count, block_len)).reshape(-1)
    key_pos = key_pos.reshape(-1)
    allowed = listed_keys[None, :] & (key_pos[None, :] <= query_pos[:, None])
    key_flat = key_sel.reshape(entry_count * block_len, kv_heads, head_dim)
    value_flat = value_sel.reshape(entry_count * block_len, kv_heads, head_dim)
    inverse_root = query_blk.shape[-1] ** (-0.5)
    scores = (
        jnp.einsum("qhgd,khd->hgqk", query_blk, key_flat, preferred_element_type=jnp.float32)
        * inverse_root
    )
    scores = jnp.where(allowed[None, None], scores, -1e30)
    row_max = jnp.max(scores, axis=3, keepdims=True)
    weights = jnp.exp(scores - row_max)
    softmax = weights / jnp.sum(weights, axis=3, keepdims=True)
    softmax_lo = softmax.astype(jnp.bfloat16)
    attended = jnp.einsum(
        "hgqk,khd->qhgd", softmax_lo, value_flat, preferred_element_type=jnp.float32
    ).astype(jnp.bfloat16)
    row_dot = jnp.einsum("qhgd,qhgd->hgq", grad_blk, attended, preferred_element_type=jnp.float32)
    dprob = jnp.einsum("qhgd,khd->hgqk", grad_blk, value_flat, preferred_element_type=jnp.float32)
    dscore = (softmax * (dprob - row_dot[..., None])).astype(jnp.bfloat16)
    query_gradient = (
        jnp.einsum("hgqk,khd->qhgd", dscore, key_flat, preferred_element_type=jnp.float32)
        * inverse_root
    ).astype(jnp.bfloat16)
    grad_key_ent = (
        jnp.einsum("hgqk,qhgd->khd", dscore, query_blk, preferred_element_type=jnp.float32)
        * inverse_root
    )
    return (query_gradient, grad_key_ent.reshape(entry_count, block_len, kv_heads, head_dim))


def per_device(query_projections, key_states, value_projections, grad_incoming, key_blocks):
    rank_ctx = lax.axis_index("ctx")
    selected_rows = query_projections.shape[1]
    output_gradient = shifted(grad_incoming, "pipe", -1)
    own_pair = (key_states[0], value_projections[0])
    key_collection = [own_pair[0]]
    value_collection = [own_pair[1]]
    passing = own_pair
    for offset in range(MAX_RANK_REACH):
        passing = from_behind((passing[0], passing[1]), "ctx", 1)
        key_collection.append(passing[0])
        value_collection.append(passing[1])
    window_width_slots = (MAX_RANK_REACH + 1) * BLOCKS_PER_RANK
    key_span = jnp.stack(key_collection).reshape(
        window_width_slots, TREE_BLOCK_SIZE, KEY_VALUE_HEADS, HEAD_SIZE
    )
    value_span = jnp.stack(value_collection).reshape(
        window_width_slots, TREE_BLOCK_SIZE, KEY_VALUE_HEADS, HEAD_SIZE
    )
    entries_all = key_blocks[0]
    listed = entries_all >= 0
    clamped = jnp.maximum(entries_all, 0)
    behind = rank_ctx - clamped // BLOCKS_PER_RANK
    window_slot = jnp.where(listed, behind * BLOCKS_PER_RANK + clamped % BLOCKS_PER_RANK, 0)
    selector = (
        (window_slot[..., None] == jnp.arange(window_width_slots, dtype=jnp.int32))
        & listed[..., None]
    ).astype(jnp.float32)
    query_block_rows = query_projections[0].reshape(
        BLOCKS_PER_RANK, TREE_BLOCK_SIZE, KEY_VALUE_HEADS, QUERY_GROUP, HEAD_SIZE
    )
    gradient_blocks = output_gradient[0].reshape(
        BLOCKS_PER_RANK, TREE_BLOCK_SIZE, KEY_VALUE_HEADS, QUERY_GROUP, HEAD_SIZE
    )
    key_window_gradient = jnp.zeros(
        (window_width_slots, TREE_BLOCK_SIZE, KEY_VALUE_HEADS, HEAD_SIZE), jnp.float32
    )
    grad_query_list = []
    for block_pos in range(BLOCKS_PER_RANK):
        first_pos = (rank_ctx * BLOCKS_PER_RANK + block_pos) * TREE_BLOCK_SIZE
        chosen_slots = window_slot[block_pos]
        query_gradient, grad_key_ent = attend_block(
            query_block_rows[block_pos],
            key_span[chosen_slots],
            value_span[chosen_slots],
            gradient_blocks[block_pos],
            entries_all[block_pos],
            first_pos,
        )
        grad_query_list.append(query_gradient)
        key_window_gradient = key_window_gradient + jnp.einsum(
            "jw,jkhd->wkhd", selector[block_pos], grad_key_ent, precision=lax.Precision.HIGHEST
        )
    grad_query_all = jnp.stack(grad_query_list).reshape(1, selected_rows, QUERY_HEADS * HEAD_SIZE)
    key_window_gradient = key_window_gradient.reshape(
        MAX_RANK_REACH + 1, selected_rows, KEY_VALUE_HEADS * HEAD_SIZE
    )
    running = key_window_gradient[MAX_RANK_REACH]
    for offset in range(MAX_RANK_REACH - 1, -1, -1):
        arrived = from_behind(running, "ctx", -1)
        running = arrived + key_window_gradient[offset]
    key_gradient = running.astype(jnp.bfloat16)[None]
    return (grad_query_all, key_gradient)


def solution(mesh):
    in_specs = (
        P("pipe", "ctx", None),
        P("pipe", "ctx", None),
        P("pipe", "ctx", None),
        P("pipe", "ctx", None),
        P("pipe", "ctx", None),
    )
    out_specs = (P("pipe", "ctx", None), P("pipe", "ctx", None))
    return jax.shard_map(
        per_device, mesh=mesh, in_specs=in_specs, out_specs=out_specs, check_vma=False
    )
```

profile of v0, /device:TPU:3, one launch (start us, length us, event | category | flops | bytes accessed | tf_op | source)
XLA Modules:
  0.0 68.5 jit_solution(18298770094060182462)
XLA Ops:
  0.6 3.7 %collective-permute-start = (bf16[128,512]{1,0:T(8,128)(2,1)}, bf16[128,512]{1,0:T(8,128)(2,1)S(1)}, u32[]{:S(2)}, u32[]{:S(2)}) collective-permute-start(bf16[128,512]{1,0:T(8,128)(2,1)} %bitcast.232), channel_id=1, source_target_pairs={{0,1},{1,2},{2,3},{3,4},{4,5},{5,6},{6,7},{8,9},{9,10},{10,11},{11... | collective-permute-start | bytes 393224 | tf_op jit(solution)/shard_map/ppermute | solution.py:24
  4.3 1.9 %collective-permute-start.2 = (bf16[128,512]{1,0:T(8,128)(2,1)}, bf16[128,512]{1,0:T(8,128)(2,1)S(1)}, u32[]{:S(2)}, u32[]{:S(2)}) collective-permute-start(bf16[128,512]{1,0:T(8,128)(2,1)} %bitcast.233), channel_id=1, source_target_pairs={{0,1},{1,2},{2,3},{3,4},{4,5},{5,6},{6,7},{8,9},{9,10},{10,11},{11... | collective-permute-start | bytes 393224 | tf_op jit(solution)/shard_map/ppermute | solution.py:24
  6.2 3.4 %collective-permute-start.4 = (bf16[1,128,4096]{2,1,0:T(8,128)(2,1)}, bf16[1,128,4096]{2,1,0:T(8,128)(2,1)}, u32[]{:S(2)}, u32[]{:S(2)}) collective-permute-start(bf16[1,128,4096]{2,1,0:T(8,128)(2,1)} %param.8), channel_id=1, source_target_pairs={{0,24},{8,0},{16,8},{24,16},{1,25},{9,1},{17,9},{25,17},{2,26},{10... | collective-permute-start | bytes 3145736 | tf_op jit(solution)/shard_map/ppermute | solution.py:18
  12.8 1.3 %slice_bitcast_fusion.3 = (bf16[8,8,32,128]{3,1,2,0:T(8,128)(2,1)S(1)}, bf16[8,8,32,128]{3,1,2,0:T(8,128)(2,1)S(1)}) fusion(bf16[1,128,4096]{2,1,0:T(8,128)(2,1)} %param.5), kind=kLoop, calls=%fused_computation.51 | loop fusion | bytes 2097152
  14.7 3.8 %collective-permute-start.1 = (bf16[128,512]{1,0:T(8,128)(2,1)S(1)}, bf16[128,512]{1,0:T(8,128)(2,1)S(1)}, u32[]{:S(2)}, u32[]{:S(2)}) collective-permute-start(bf16[128,512]{1,0:T(8,128)(2,1)S(1)} %collective-permute-done), channel_id=1, source_target_pairs={{0,1},{1,2},{2,3},{3,4},{4,5},{5,6},{6,7},{8,9},{9,10},{10,11},{11... | collective-permute-start | bytes 393224 | tf_op jit(solution)/shard_map/ppermute | solution.py:24
  18.6 1.0 %copy.55 = bf16[8,8,32,128]{3,2,1,0:T(8,128)(2,1)} copy(bf16[8,8,32,128]{3,1,2,0:T(8,128)(2,1)S(1)} %get-tuple-element.6) | data formatting | bytes 1048576
  19.6 1.9 %collective-permute-start.3 = (bf16[128,512]{1,0:T(8,128)(2,1)S(1)}, bf16[128,512]{1,0:T(8,128)(2,1)S(1)}, u32[]{:S(2)}, u32[]{:S(2)}) collective-permute-start(bf16[128,512]{1,0:T(8,128)(2,1)S(1)} %collective-permute-done.2), channel_id=1, source_target_pairs={{0,1},{1,2},{2,3},{3,4},{4,5},{5,6},{6,7},{8,9},{9,10},{10,11},{11... | collective-permute-start | bytes 393224 | tf_op jit(solution)/shard_map/ppermute | solution.py:24
  22.4 1.5 %fusion.57 = (f32[4,8,64]{2,1,0:T(8,128)S(1)}, f32[4,8,64,128]{3,2,1,0:T(8,128)}) fusion(bf16[128,4,128,1]{2,0,3,1:T(8,128)(2,1)S(1)} %bitcast.216, pred[64,128]{1,0:T(8,128)(4,1)S(1)} %compare_and_fusion.1, bf16[64,4,8,128]{3,2,1,0:T(8,128)(2,1)S(1)} %bitcast.209), kind=kOutput, calls=%fused_computation.101 | convolution fusion | flops 68157568 | bytes 1720320 | tf_op jit(solution)/shard_map/sub | solution.py:45
  25.7 1.3 %gather_fusion.3 = bf16[2,64,4,128]{3,2,1,0:T(4,128)(2,1)} fusion(bf16[6,64,4,128]{3,2,1,0:T(4,128)(2,1)S(1)} %reshape.319, s32[1024]{0:T(1024)S(1)} %get-tuple-element.19), kind=kCustom, calls=%fused_computation.3 | custom fusion | bytes 262152 | tf_op jit(solution)/shard_map/gather | solution.py:109
  27.1 3.7 %fusion.26 = bf16[4,128,8,64]{1,3,2,0:T(8,128)(2,1)S(1)} fusion(bf16[128,4,128,1]{2,0,3,1:T(8,128)(2,1)S(1)} %bitcast.230, f32[4,8,64]{2,1,0:T(8,128)S(1)} %get-tuple-element.17, f32[4,8,64,128]{3,2,1,0:T(8,128)S(1)} %fusion.13), kind=kOutput, calls=%fused_computation.48 | convolution fusion | flops 67897472 | bytes 1712128 | tf_op jit(solution)/shard_map/hgqk,khd->qhgd/dot_general | solution.py:48
  31.5 2.1 %copy.37 = f32[4,8,64,128]{3,1,0,2:T(8,128)} copy(f32[4,8,64,128]{2,1,3,0:T(8,128)S(1)} %bitcast_convert_fusion.1) | data formatting | bytes 2097152
  33.6 1.5 %fusion.54 = (f32[4,8,64]{2,1,0:T(8,128)S(1)}, f32[4,8,64,128]{3,2,1,0:T(8,128)}) fusion(bf16[128,4,128,1]{2,0,3,1:T(8,128)(2,1)S(1)} %bitcast.219, pred[64,128]{1,0:T(8,128)(4,1)S(1)} %compare_and_fusion, bf16[64,4,8,128]{3,2,1,0:T(8,128)(2,1)S(1)} %bitcast.206), kind=kOutput, calls=%fused_computation.100 | convolution fusion | flops 68157568 | bytes 1720320 | tf_op jit(solution)/shard_map/sub | solution.py:45
  35.5 3.7 %fusion.24 = bf16[4,128,8,64]{1,3,2,0:T(8,128)(2,1)S(1)} fusion(bf16[128,4,128,1]{2,0,3,1:T(8,128)(2,1)S(1)} %bitcast.228, f32[4,8,64]{2,1,0:T(8,128)S(1)} %get-tuple-element.15, f32[4,8,64,128]{3,2,1,0:T(8,128)S(1)} %fusion.9), kind=kOutput, calls=%fused_computation.44 | convolution fusion | flops 67897472 | bytes 1712128 | tf_op jit(solution)/shard_map/hgqk,khd->qhgd/dot_general | solution.py:48
  39.9 1.2 %copy.47 = f32[4,8,64,128]{3,1,0,2:T(8,128)S(1)} copy(f32[4,8,64,128]{2,1,3,0:T(8,128)S(1)} %bitcast_convert_fusion) | data formatting | bytes 2097152
  41.1 1.4 %slice_bitcast_fusion.1 = (bf16[8,8,32,128]{3,1,2,0:T(8,128)(2,1)S(1)}, bf16[8,8,32,128]{3,1,2,0:T(8,128)(2,1)S(1)}) fusion(bf16[1,128,4096]{2,1,0:T(8,128)(2,1)} %collective-permute-done.4), kind=kLoop, calls=%fused_computation.41 | loop fusion | bytes 2097152
  43.2 2.0 %fusion.14 = bf16[4,8,64,128]{3,2,1,0:T(8,128)(2,1)S(1)} fusion(bf16[128,4,128,1]{2,0,3,1:T(8,128)(2,1)S(1)} %bitcast.231, bf16[64,4,8,128]{3,2,1,0:T(8,128)(2,1)S(1)} %bitcast.213, f32[4,8,64]{2,1,0:T(8,128)S(1)} %copy.38, f32[4,8,64,128]{3,2,1,0:T(8,128)} %get-tuple-element.18, f32[4,8,64]{2,1,0:T(8,128)S(1)} %copy-done.13), kind=kOutput, calls=%fused_computation.25 | convolution fusion | flops 68157440 | bytes 2244608 | tf_op jit(solution)/shard_map/qhgd,khd->hgqk/dot_general | solution.py:52
  46.2 1.9 %fusion.15 = bf16[4,8,64,128]{3,2,1,0:T(8,128)(2,1)S(1)} fusion(bf16[128,4,128,1]{2,0,3,1:T(8,128)(2,1)S(1)} %bitcast.229, bf16[64,4,8,128]{3,2,1,0:T(8,128)(2,1)S(1)} %bitcast.215, f32[4,8,64]{2,1,0:T(8,128)S(1)} %copy.48, f32[4,8,64,128]{3,2,1,0:T(8,128)} %get-tuple-element.16, f32[4,8,64]{2,1,0:T(8,128)S(1)} %copy-done.15), kind=kOutput, calls=%fused_computation.26 | convolution fusion | flops 68157440 | bytes 2244608 | tf_op jit(solution)/shard_map/qhgd,khd->hgqk/dot_general | solution.py:52
  48.5 0.8 %fusion.34 = f32[6,64,4,128]{3,0,2,1:T(8,128)S(1)} fusion(f32[2,64,4,128]{3,1,0,2:T(8,128)S(1)} %bitcast.225, pred[2,2,6]{2,1,0:T(4,128)(4,1)S(1)} %compare_and_fusion.2), kind=kOutput, calls=%fused_computation.63 | convolution fusion | flops 4718592 | bytes 1049088 | tf_op jit(solution)/shard_map/jw,jkhd->wkhd/dot_general | solution.py:115
  49.3 0.8 %convolution_add_fusion = f32[6,64,4,128]{3,0,2,1:T(8,128)S(1)} fusion(f32[6,64,4,128]{3,0,2,1:T(8,128)S(1)} %fusion.34, f32[2,64,4,128]{3,1,0,2:T(8,128)S(1)} %bitcast.226, pred[2,2,6]{2,1,0:T(4,128)(4,1)S(1)} %compare_and_fusion.2), kind=kOutput, calls=%fused_computation.10 | convolution fusion | flops 4915200 | bytes 2097664 | tf_op jit(solution)/shard_map/jw,jkhd->wkhd/dot_general | solution.py:115
  50.5 2.4 %collective-permute-start.5 = (f32[128,512]{1,0:T(8,128)S(1)}, f32[128,512]{1,0:T(8,128)S(1)}, u32[]{:S(2)}, u32[]{:S(2)}) collective-permute-start(f32[128,512]{1,0:T(8,128)S(1)} %bitcast.227), channel_id=1, source_target_pairs={{1,0},{2,1},{3,2},{4,3},{5,4},{6,5},{7,6},{9,8},{10,9},{11,10},{12... | collective-permute-start | bytes 786440 | tf_op jit(solution)/shard_map/ppermute | solution.py:24
  53.4 5.7 %collective-permute-done.5 = f32[128,512]{1,0:T(8,128)S(1)} collective-permute-done((f32[128,512]{1,0:T(8,128)S(1)}, f32[128,512]{1,0:T(8,128)S(1)}, u32[]{:S(2)}, u32[]{:S(2)}) %collective-permute-start.5) | collective-permute-done | bytes 262176 | tf_op jit(solution)/shard_map/ppermute | solution.py:24
  59.2 1.9 %collective-permute-start.6 = (f32[128,512]{1,0:T(8,128)S(1)}, f32[128,512]{1,0:T(8,128)S(1)}, u32[]{:S(2)}, u32[]{:S(2)}) collective-permute-start(f32[128,512]{1,0:T(8,128)S(1)} %bitcast_add_fusion.1), channel_id=1, source_target_pairs={{1,0},{2,1},{3,2},{4,3},{5,4},{6,5},{7,6},{9,8},{10,9},{11,10},{12... | collective-permute-start | bytes 786440 | tf_op jit(solution)/shard_map/ppermute | solution.py:24
  62.2 1.3 %reshape.323 = bf16[1,128,4096]{2,1,0:T(8,128)(2,1)} reshape(bf16[2,64,4,8,128]{4,3,2,1,0:T(8,128)(2,1)S(1)} %copy.21) | data formatting | bytes 2097152 | tf_op jit(solution)/shard_map/reshape | solution.py:118
  63.5 4.3 %collective-permute-done.6 = f32[128,512]{1,0:T(8,128)S(1)} collective-permute-done((f32[128,512]{1,0:T(8,128)S(1)}, f32[128,512]{1,0:T(8,128)S(1)}, u32[]{:S(2)}, u32[]{:S(2)}) %collective-permute-start.6) | collective-permute-done | bytes 262176 | tf_op jit(solution)/shard_map/ppermute | solution.py:24
  (92 shorter events, 12.9 us)
Async XLA Ops:
  0.6 14.0 %collective-permute-start = (bf16[128,512]{1,0:T(8,128)(2,1)}, bf16[128,512]{1,0:T(8,128)(2,1)S(1)}, u32[]{:S(2)}, u32[]{:S(2)}) collective-permute-start(bf16[128,512]{1,0:T(8,128)(2,1)} %bitcast.232), channel_id=1, source_target_pairs={{0,1},{1,2},{2,3},{3,4},{4,5},{5,6},{6,7},{8,9},{9,10},{10,11},{11... | collective-permute-start | bytes 393224 | tf_op jit(solution)/shard_map/ppermute | solution.py:24
  4.3 15.2 %collective-permute-start.2 = (bf16[128,512]{1,0:T(8,128)(2,1)}, bf16[128,512]{1,0:T(8,128)(2,1)S(1)}, u32[]{:S(2)}, u32[]{:S(2)}) collective-permute-start(bf16[128,512]{1,0:T(8,128)(2,1)} %bitcast.233), channel_id=1, source_target_pairs={{0,1},{1,2},{2,3},{3,4},{4,5},{5,6},{6,7},{8,9},{9,10},{10,11},{11... | collective-permute-start | bytes 393224 | tf_op jit(solution)/shard_map/ppermute | solution.py:24
  6.2 34.9 %collective-permute-start.4 = (bf16[1,128,4096]{2,1,0:T(8,128)(2,1)}, bf16[1,128,4096]{2,1,0:T(8,128)(2,1)}, u32[]{:S(2)}, u32[]{:S(2)}) collective-permute-start(bf16[1,128,4096]{2,1,0:T(8,128)(2,1)} %param.8), channel_id=1, source_target_pairs={{0,24},{8,0},{16,8},{24,16},{1,25},{9,1},{17,9},{25,17},{2,26},{10... | collective-permute-start | bytes 3145736 | tf_op jit(solution)/shard_map/ppermute | solution.py:18
  12.8 8.7 %copy-start.10 = (bf16[1,128,512]{2,1,0:T(8,128)(2,1)S(1)}, bf16[1,128,512]{2,1,0:T(8,128)(2,1)}, u32[]{:S(2)}) copy-start(bf16[1,128,512]{2,1,0:T(8,128)(2,1)} %param.6) | copy-start | bytes 393220
  14.7 6.8 %collective-permute-start.1 = (bf16[128,512]{1,0:T(8,128)(2,1)S(1)}, bf16[128,512]{1,0:T(8,128)(2,1)S(1)}, u32[]{:S(2)}, u32[]{:S(2)}) collective-permute-start(bf16[128,512]{1,0:T(8,128)(2,1)S(1)} %collective-permute-done), channel_id=1, source_target_pairs={{0,1},{1,2},{2,3},{3,4},{4,5},{5,6},{6,7},{8,9},{9,10},{10,11},{11... | collective-permute-start | bytes 393224 | tf_op jit(solution)/shard_map/ppermute | solution.py:24
  18.5 5.3 %copy-start.3 = (bf16[8,8,32,128]{3,2,1,0:T(8,128)(2,1)}, bf16[8,8,32,128]{3,2,1,0:T(8,128)(2,1)S(1)}, u32[]{:S(2)}) copy-start(bf16[8,8,32,128]{3,2,1,0:T(8,128)(2,1)S(1)} %copy.53) | copy-start | bytes 1572868
  19.6 4.7 %collective-permute-start.3 = (bf16[128,512]{1,0:T(8,128)(2,1)S(1)}, bf16[128,512]{1,0:T(8,128)(2,1)S(1)}, u32[]{:S(2)}, u32[]{:S(2)}) collective-permute-start(bf16[128,512]{1,0:T(8,128)(2,1)S(1)} %collective-permute-done.2), channel_id=1, source_target_pairs={{0,1},{1,2},{2,3},{3,4},{4,5},{5,6},{6,7},{8,9},{9,10},{10,11},{11... | collective-permute-start | bytes 393224 | tf_op jit(solution)/shard_map/ppermute | solution.py:24
  22.3 1.9 %copy-start.11 = (bf16[1,128,512]{2,1,0:T(8,128)(2,1)S(1)}, bf16[1,128,512]{2,1,0:T(8,128)(2,1)}, u32[]{:S(2)}) copy-start(bf16[1,128,512]{2,1,0:T(8,128)(2,1)} %param.7) | copy-start | bytes 393220
  23.9 3.2 %copy-start.12 = (f32[4,8,64]{2,1,0:T(8,128)}, f32[4,8,64]{2,1,0:T(8,128)S(1)}, u32[]{:S(2)}) copy-start(f32[4,8,64]{2,1,0:T(8,128)S(1)} %get-tuple-element.17) | copy-start | bytes 24580
  27.1 3.7 %copy-start.8 = (bf16[2,64,4,128]{3,1,0,2:T(8,128)(2,1)}, bf16[2,64,4,128]{3,1,0,2:T(8,128)(2,1)S(1)}, u32[]{:S(2)}) copy-start(bf16[2,64,4,128]{3,1,0,2:T(8,128)(2,1)S(1)} %copy.15) | copy-start | bytes 393220
  31.5 2.1 %copy-start.7 = (bf16[2,64,4,128]{3,2,1,0:T(4,128)(2,1)S(1)}, bf16[2,64,4,128]{3,2,1,0:T(4,128)(2,1)}, u32[]{:S(2)}) copy-start(bf16[2,64,4,128]{3,2,1,0:T(4,128)(2,1)} %gather_fusion.3) | copy-start | bytes 393220
  31.5 2.1 %copy-start.1 = (bf16[8,8,32,128]{3,2,1,0:T(8,128)(2,1)S(1)}, bf16[8,8,32,128]{3,2,1,0:T(8,128)(2,1)}, u32[]{:S(2)}) copy-start(bf16[8,8,32,128]{3,2,1,0:T(8,128)(2,1)} %copy.55) | copy-start | bytes 1572868
  35.2 4.0 %copy-start.14 = (f32[4,8,64]{2,1,0:T(8,128)}, f32[4,8,64]{2,1,0:T(8,128)S(1)}, u32[]{:S(2)}) copy-start(f32[4,8,64]{2,1,0:T(8,128)S(1)} %get-tuple-element.15) | copy-start | bytes 24580
  41.1 1.5 %copy-start = (f32[4,8,64,128]{3,1,0,2:T(8,128)S(1)}, f32[4,8,64,128]{3,1,0,2:T(8,128)}, u32[]{:S(2)}) copy-start(f32[4,8,64,128]{3,1,0,2:T(8,128)} %copy.37) | copy-start | bytes 3145732
  41.1 2.1 %copy-start.9 = (bf16[2,64,4,128]{3,1,0,2:T(8,128)(2,1)S(1)}, bf16[2,64,4,128]{3,1,0,2:T(8,128)(2,1)}, u32[]{:S(2)}) copy-start(bf16[2,64,4,128]{3,1,0,2:T(8,128)(2,1)} %copy-done.8) | copy-start | bytes 393220
  41.1 2.1 %copy-start.13 = (f32[4,8,64]{2,1,0:T(8,128)S(1)}, f32[4,8,64]{2,1,0:T(8,128)}, u32[]{:S(2)}) copy-start(f32[4,8,64]{2,1,0:T(8,128)} %copy-done.12) | copy-start | bytes 24580
  43.2 2.0 %copy-start.4 = (bf16[8,8,32,128]{3,2,1,0:T(8,128)(2,1)S(1)}, bf16[8,8,32,128]{3,2,1,0:T(8,128)(2,1)}, u32[]{:S(2)}) copy-start(bf16[8,8,32,128]{3,2,1,0:T(8,128)(2,1)} %copy-done.3) | copy-start | bytes 1572868
  45.2 1.1 %copy-start.5 = (bf16[4,8,64,128]{3,2,1,0:T(8,128)(2,1)}, bf16[4,8,64,128]{3,2,1,0:T(8,128)(2,1)S(1)}, u32[]{:S(2)}) copy-start(bf16[4,8,64,128]{3,2,1,0:T(8,128)(2,1)S(1)} %fusion.14) | copy-start | bytes 1572868
  45.2 1.1 %copy-start.15 = (f32[4,8,64]{2,1,0:T(8,128)S(1)}, f32[4,8,64]{2,1,0:T(8,128)}, u32[]{:S(2)}) copy-start(f32[4,8,64]{2,1,0:T(8,128)} %copy-done.14) | copy-start | bytes 24580
  46.2 1.9 %copy-start.2 = (bf16[8,8,32,128]{3,2,1,0:T(8,128)(2,1)S(1)}, bf16[8,8,32,128]{3,2,1,0:T(8,128)(2,1)}, u32[]{:S(2)}) copy-start(bf16[8,8,32,128]{3,2,1,0:T(8,128)(2,1)} %copy.55) | copy-start | bytes 1572868
  50.2 3.0 %copy-start.6 = (bf16[4,8,64,128]{3,2,1,0:T(8,128)(2,1)S(1)}, bf16[4,8,64,128]{3,2,1,0:T(8,128)(2,1)}, u32[]{:S(2)}) copy-start(bf16[4,8,64,128]{3,2,1,0:T(8,128)(2,1)} %copy-done.5) | copy-start | bytes 1572868
  50.5 8.6 %collective-permute-start.5 = (f32[128,512]{1,0:T(8,128)S(1)}, f32[128,512]{1,0:T(8,128)S(1)}, u32[]{:S(2)}, u32[]{:S(2)}) collective-permute-start(f32[128,512]{1,0:T(8,128)S(1)} %bitcast.227), channel_id=1, source_target_pairs={{1,0},{2,1},{3,2},{4,3},{5,4},{6,5},{7,6},{9,8},{10,9},{11,10},{12... | collective-permute-start | bytes 786440 | tf_op jit(solution)/shard_map/ppermute | solution.py:24
  59.2 8.6 %collective-permute-start.6 = (f32[128,512]{1,0:T(8,128)S(1)}, f32[128,512]{1,0:T(8,128)S(1)}, u32[]{:S(2)}, u32[]{:S(2)}) collective-permute-start(f32[128,512]{1,0:T(8,128)S(1)} %bitcast_add_fusion.1), channel_id=1, source_target_pairs={{1,0},{2,1},{3,2},{4,3},{5,4},{6,5},{7,6},{9,8},{10,9},{11,10},{12... | collective-permute-start | bytes 786440 | tf_op jit(solution)/shard_map/ppermute | solution.py:24
where the time goes:
time: 68.9 us; the launch traced here: 68.5 us
  starting transfers between devices  19 us (28%)
  matrix products  17.9 us (26%)
  local copies, waits for them, and re-layouts  15.1 us (22%)
  waiting for transfers between devices  10 us (15%)
  other arithmetic  5.31 us (8%)
  between operations  1.17 us (2%)
    ppermute x6, starting transfers between devices, from_behind(): return lax.ppermute(array, axis, pairs)  15.6 us
    ppermute x6, waiting for transfers between devices, from_behind(): return lax.ppermute(array, axis, pairs)  10 us
    dot_general x2, matrix products, attend_block(): jnp.einsum('hgqk,khd->qhgd', softmax_lo, value_flat, preferred_element_ty...  7.33 us
    unnamed x41, local copies, waits for them, and re-layouts  7.28 us
    dot_general x2, matrix products, attend_block(): jnp.einsum('qhgd,khd->hgqk', grad_blk, value_flat, preferred_element_type...  3.84 us
    ppermute x1, starting transfers between devices, shifted(): return lax.ppermute(value, axis, pairs)  3.37 us
    sub x2, matrix products, attend_block(): weights = jnp.exp(scores - row_max)  3.05 us
    gather x4, local copies, waits for them, and re-layouts, per_device(): value_span[chosen_slots]  2.02 us
  transfers between devices with their start and end apart: 7, of which 2 were waited for; matrix products, arithmetic and copies ran while one was open for 41% of the time, Pallas kernels for 0%

commit v1 on v0

v1 whole, which is shorter than its diff:
```python
import functools

import jax
import jax.numpy as jnp
from jax import lax
from jax.experimental import pallas as pl
from jax.experimental.pallas import tpu as pltpu
from jax.sharding import PartitionSpec as P

HEADS = 32
GROUPS = 4
SIZE = 128
BLOCK = 64
SHARE = 8
BLOCKS = 2
REACH = 2
MESH = pl.DeviceIdType.MESH
NEG = -1e30


def stacked(ref, block, group):
    rows = pl.ds(block * BLOCK, BLOCK)
    return jnp.concatenate(
        [
            ref[rows, pl.ds(pl.multiple_of(group * SHARE * SIZE, SIZE) + h * SIZE, SIZE)]
            for h in range(SHARE)
        ],
        axis=0,
    )


def nt(a, b):
    return lax.dot_general(a, b, (((1,), (1,)), ((), ())), preferred_element_type=jnp.float32)


def tn(a, b):
    return lax.dot_general(a, b, (((0,), (0,)), ((), ())), preferred_element_type=jnp.float32)


def kernel(
    pipes, ranks, entries, q_hbm, k_hbm, v_hbm, g_hbm, dq_hbm, dk_hbm,
    qbuf, gbuf, kwin, vwin, kpar, vpar, prob, dqbuf, own, msg, arrived, dkbuf,
    load_sem, halo_send, halo_recv, grad_send, grad_recv, msg_send, msg_recv, out_sem,
):
    pipe = lax.axis_index("pipe")
    rank = lax.axis_index("ctx")
    rows = BLOCKS * BLOCK
    narrow = GROUPS * SIZE
    scale = SIZE**-0.5

    def ctx_at(step):
        return (pipe, lax.rem(rank + step + ranks, ranks))

    def pipe_at(step):
        return (lax.rem(pipe + step + pipes, pipes), rank)

    barrier = pltpu.get_barrier_semaphore()
    peers = [pipe_at(-1), pipe_at(1), ctx_at(1), ctx_at(2), ctx_at(-1), ctx_at(-2)]
    for peer in peers:
        pl.semaphore_signal(barrier, inc=1, device_id=peer, device_id_type=MESH)

    last = pl.ds(REACH * rows, rows)
    loads = [
        pltpu.make_async_copy(q_hbm, qbuf, load_sem.at[0]),
        pltpu.make_async_copy(k_hbm, kwin.at[last], load_sem.at[1]),
        pltpu.make_async_copy(v_hbm, vwin.at[last], load_sem.at[2]),
    ]
    for load in loads:
        load.start()
    pl.semaphore_wait(barrier, len(peers))

    halos = []
    for reach in (1, 2):
        place = pl.ds((REACH - reach) * rows, rows)
        for which, (source, window) in enumerate(((k_hbm, kwin), (v_hbm, vwin))):
            halos.append(
                pltpu.make_async_remote_copy(
                    src_ref=source,
                    dst_ref=window.at[place],
                    send_sem=halo_send.at[reach - 1, which],
                    recv_sem=halo_recv.at[reach - 1, which],
                    device_id=ctx_at(reach),
                    device_id_type=MESH,
                )
            )

    def grad_copy(group, block):
        part = pl.ds(block * BLOCK, BLOCK)
        lanes = pl.ds(group * SHARE * SIZE, SHARE * SIZE)
        return pltpu.make_async_remote_copy(
            src_ref=g_hbm.at[part, lanes],
            dst_ref=gbuf.at[part, lanes],
            send_sem=grad_send.at[group, block],
            recv_sem=grad_recv.at[group, block],
            device_id=pipe_at(-1),
            device_id_type=MESH,
        )

    def msg_copy(group, reach):
        return pltpu.make_async_remote_copy(
            src_ref=msg.at[reach - 1, group],
            dst_ref=arrived.at[reach - 1, group],
            send_sem=msg_send.at[reach - 1, group],
            recv_sem=msg_recv.at[reach - 1, group],
            device_id=ctx_at(-reach),
            device_id_type=MESH,
        )

    grads = [[grad_copy(group, block) for block in range(BLOCKS)] for group in range(GROUPS)]
    grads[0][0].start()
    for halo in halos:
        halo.start()
    for group in range(GROUPS):
        for block in range(BLOCKS):
            if (group, block) != (0, 0):
                grads[group][block].start()
    for load in loads:
        load.wait()
    for halo in halos:
        halo.wait_recv()

    def slot_of(block, shape):
        entry = jnp.full(shape, entries[block, 1], jnp.int32)
        return jnp.where(entry >= 0, entry - (rank - REACH) * BLOCKS, -1)

    for block in range(BLOCKS):
        wide = slot_of(block, (BLOCK, narrow))
        for window, parents in ((kwin, kpar), (vwin, vpar)):
            total = jnp.zeros((BLOCK, narrow), jnp.float32)
            for slot in range(block, REACH * BLOCKS + block):
                held = window[pl.ds(slot * BLOCK, BLOCK), :].astype(jnp.float32)
                total = jnp.where(wide == slot, held, total)
            parents[block] = total.astype(jnp.bfloat16)

    def chosen(window, parents, group, block):
        lanes = pl.ds(pl.multiple_of(group * SIZE, SIZE), SIZE)
        mine = window[pl.ds(REACH * rows + block * BLOCK, BLOCK), lanes]
        return jnp.concatenate([mine, parents[block, :, lanes]], axis=0)

    slots = [slot_of(block, (BLOCK, SIZE)) for block in range(BLOCKS)]
    width = SHARE * BLOCK
    key_row = lax.broadcasted_iota(jnp.int32, (BLOCK, width), 0)
    query_row = lax.rem(lax.broadcasted_iota(jnp.int32, (BLOCK, width), 1), BLOCK)

    def forward(group, carry):
        for block in range(BLOCKS):
            scores = nt(chosen(kwin, kpar, group, block), stacked(qbuf, block, group))
            mine = jnp.where(key_row <= query_row, scores[:BLOCK], NEG)
            parent = jnp.where(slot_of(block, (BLOCK, width)) >= 0, scores[BLOCK:], NEG)
            top = jnp.maximum(
                jnp.max(mine, axis=0, keepdims=True), jnp.max(parent, axis=0, keepdims=True)
            )
            mine = jnp.exp((mine - top) * scale)
            parent = jnp.exp((parent - top) * scale)
            total = jnp.sum(mine, axis=0, keepdims=True) + jnp.sum(parent, axis=0, keepdims=True)
            inverse = 1.0 / total
            prob[group, block, :BLOCK] = mine * inverse
            prob[group, block, BLOCK:] = parent * inverse
        return carry

    lax.fori_loop(0, GROUPS, forward, 0)

    def backward(group, block):
        soft = prob[group, block]
        dprob = nt(chosen(vwin, vpar, group, block), stacked(gbuf, block, group))
        dot = jnp.sum(soft * dprob, axis=0, keepdims=True)
        dscore = (soft * (dprob - dot)).astype(jnp.bfloat16)
        dkey = (
            jnp.dot(dscore, stacked(qbuf, block, group), preferred_element_type=jnp.float32) * scale
        )
        return dscore, dkey

    def query_part(group, block, dscore):
        dquery = (tn(dscore, chosen(kwin, kpar, group, block)) * scale).astype(jnp.bfloat16)
        for h in range(SHARE):
            dqbuf[pl.ds(block * BLOCK, BLOCK), pl.ds((group * SHARE + h) * SIZE, SIZE)] = dquery[
                h * BLOCK : (h + 1) * BLOCK
            ]

    writes = []

    def write_query(group, block):
        part = pl.ds(block * BLOCK, BLOCK)
        lanes = pl.ds(group * SHARE * SIZE, SHARE * SIZE)
        write = pltpu.make_async_copy(
            dqbuf.at[part, lanes], dq_hbm.at[part, lanes], out_sem.at[group * BLOCKS + block]
        )
        write.start()
        writes.append(write)

    for group in range(GROUPS):
        grads[group][0].wait_recv()
        dscore0, dkey0 = backward(group, 0)
        query_part(group, 0, dscore0)
        write_query(group, 0)
        grads[group][1].wait_recv()
        dscore1, dkey1 = backward(group, 1)
        parent0, parent1 = dkey0[BLOCK:], dkey1[BLOCK:]

        def at_slot(slot):
            total = jnp.zeros((BLOCK, SIZE), jnp.float32)
            for block, parent in enumerate((parent0, parent1)):
                if block <= slot < REACH * BLOCKS + block:
                    total = total + jnp.where(slots[block] == slot, parent, 0.0)
            return total

        for reach in (2, 1):
            first = (REACH - reach) * BLOCKS
            for block in range(BLOCKS):
                msg[reach - 1, group, pl.ds(block * BLOCK, BLOCK)] = at_slot(first + block).astype(
                    jnp.bfloat16
                )
            msg_copy(group, reach).start()
        own[group, :BLOCK] = dkey0[:BLOCK] + at_slot(REACH * BLOCKS)
        own[group, BLOCK:] = dkey1[:BLOCK]
        query_part(group, 1, dscore1)
        write_query(group, 1)

    for group in range(GROUPS):
        total = own[group]
        for reach in (1, 2):
            msg_copy(group, reach).wait_recv()
            total = total + arrived[reach - 1, group].astype(jnp.float32)
        dkbuf[:, pl.ds(group * SIZE, SIZE)] = total.astype(jnp.bfloat16)
    write = pltpu.make_async_copy(dkbuf, dk_hbm, out_sem.at[GROUPS * BLOCKS])
    write.start()
    writes.append(write)

    for halo in halos:
        halo.wait_send()
    for group in range(GROUPS):
        for block in range(BLOCKS):
            grads[group][block].wait_send()
        for reach in (1, 2):
            msg_copy(group, reach).wait_send()
    for write in writes:
        write.wait()


def solution(mesh):
    pipes, ranks = mesh.shape["pipe"], mesh.shape["ctx"]

    def per_device(query, key, value, grad, key_blocks):
        rows = query.shape[1]
        wide, narrow = query.shape[2], key.shape[2]
        anywhere = pl.BlockSpec(memory_space=pl.ANY)
        dma = pltpu.SemaphoreType.DMA
        dq, dk = pl.pallas_call(
            functools.partial(kernel, pipes, ranks),
            out_shape=(
                jax.ShapeDtypeStruct((rows, wide), jnp.bfloat16),
                jax.ShapeDtypeStruct((rows, narrow), jnp.bfloat16),
            ),
            in_specs=[pl.BlockSpec(memory_space=pltpu.SMEM)] + [anywhere] * 4,
            out_specs=(anywhere, anywhere),
            scratch_shapes=[
                pltpu.VMEM((rows, wide), jnp.bfloat16),
                pltpu.VMEM((rows, wide), jnp.bfloat16),
                pltpu.VMEM(((REACH + 1) * rows, narrow), jnp.bfloat16),
                pltpu.VMEM(((REACH + 1) * rows, narrow), jnp.bfloat16),
                pltpu.VMEM((BLOCKS, BLOCK, narrow), jnp.bfloat16),
                pltpu.VMEM((BLOCKS, BLOCK, narrow), jnp.bfloat16),
                pltpu.VMEM((GROUPS, BLOCKS, 2 * BLOCK, SHARE * BLOCK), jnp.float32),
                pltpu.VMEM((rows, wide), jnp.bfloat16),
                pltpu.VMEM((GROUPS, rows, SIZE), jnp.float32),
                pltpu.VMEM((REACH, GROUPS, rows, SIZE), jnp.bfloat16),
                pltpu.VMEM((REACH, GROUPS, rows, SIZE), jnp.bfloat16),
                pltpu.VMEM((rows, narrow), jnp.bfloat16),
                dma((3,)),
                dma((REACH, 2)),
                dma((REACH, 2)),
                dma((GROUPS, BLOCKS)),
                dma((GROUPS, BLOCKS)),
                dma((REACH, GROUPS)),
                dma((REACH, GROUPS)),
                dma((GROUPS * BLOCKS + 1,)),
            ],
            compiler_params=pltpu.CompilerParams(
                collective_id=0, has_side_effects=True, vmem_limit_bytes=32 * 1024 * 1024
            ),
            cost_estimate=pl.CostEstimate(
                flops=700_000_000, bytes_accessed=4_000_000, transcendentals=600_000
            ),
        )(key_blocks[0], query[0], key[0], value[0], grad[0])
        return dq[None], dk[None]

    spec = P("pipe", "ctx", None)
    return jax.shard_map(
        per_device, mesh=mesh, in_specs=(spec,) * 5, out_specs=(spec, spec), check_vma=False
    )
```

time: 68.9 us -> 40.5 us (0.59)
  the two profiles are of different devices: /device:TPU:3 before, /device:TPU:0 now
where the time goes in v1:
time: 40.5 us; the launch traced here: 40.2 us
  Pallas kernels  33 us (81%)
  local copies, waits for them, and re-layouts  6.56 us (16%)
  between operations  0.65 us (2%)
    pallas_call x1, Pallas kernels, per_device(): pl.pallas_call(functools.partial(kernel, pipes, ranks), out_shape=(jax.Sh...  33 us
    unnamed x12, local copies, waits for them, and re-layouts  6.56 us

profile of v1, /device:TPU:0, one launch (start us, length us, event | category | flops | bytes accessed | tf_op | source)
XLA Modules:
  0.0 40.2 jit_solution(11672953298209893440)
XLA Ops:
  0.6 0.0 copy-start.4
  0.6 0.7 %copy-done.4 = s32[1,2,2]{2,1,0:T(2,128)S(1)} copy-done((s32[1,2,2]{2,1,0:T(2,128)S(1)}, s32[1,2,2]{2,1,0:T(2,128)}, u32[]{:S(2)}) %copy-start.4) | copy-done | bytes 40
  1.3 0.0 copy-start
  1.3 1.2 %copy-done = bf16[1,128,4096]{2,1,0:T(8,128)(2,1)S(1)} copy-done((bf16[1,128,4096]{2,1,0:T(8,128)(2,1)S(1)}, bf16[1,128,4096]{2,1,0:T(8,128)(2,1)}, u32[]{:S(2)}) %copy-start) | copy-done | bytes 1048600
  2.5 0.0 copy-start.1
  2.5 1.2 %copy-done.1 = bf16[1,128,4096]{2,1,0:T(8,128)(2,1)S(1)} copy-done((bf16[1,128,4096]{2,1,0:T(8,128)(2,1)S(1)}, bf16[1,128,4096]{2,1,0:T(8,128)(2,1)}, u32[]{:S(2)}) %copy-start.1) | copy-done | bytes 1048600
  3.8 0.0 copy-start.2
  3.8 0.9 %copy-done.2 = bf16[1,128,512]{2,1,0:T(8,128)(2,1)S(1)} copy-done((bf16[1,128,512]{2,1,0:T(8,128)(2,1)S(1)}, bf16[1,128,512]{2,1,0:T(8,128)(2,1)}, u32[]{:S(2)}) %copy-start.2) | copy-done | bytes 131096
  4.7 0.0 copy-start.3
  4.7 0.9 %copy-done.3 = bf16[1,128,512]{2,1,0:T(8,128)(2,1)S(1)} copy-done((bf16[1,128,512]{2,1,0:T(8,128)(2,1)S(1)}, bf16[1,128,512]{2,1,0:T(8,128)(2,1)}, u32[]{:S(2)}) %copy-start.3) | copy-done | bytes 131096
  5.6 33.0 %shard_map.68 = (bf16[128,4096]{1,0:T(8,128)(2,1)S(1)}, bf16[128,512]{1,0:T(8,128)(2,1)S(1)}) custom-call(s32[2,2]{1,0:T(2,128)S(1)} %bitcast.13, bf16[128,4096]{1,0:T(8,128)(2,1)S(1)} %bitcast.9, bf16[128,512]{1,0:T(8,128)(2,1)S(1)} %bitcast.11, bf16[128,512]{1,0:T(8,128)(2,1)S(1)} %bitcast.12, bf16[128,4096]{1,0:T(8,128)(2,1)S(1)} %bitcast.10), custom_call_target="tpu_custom_call" | custom-call | flops 700000000 | bytes 4000000 | tf_op jit(solution)/shard_map/pallas_call | solution.py:248
  38.6 1.0 %copy.9 = bf16[1,128,4096]{2,1,0:T(8,128)(2,1)} copy(bf16[1,128,4096]{2,1,0:T(8,128)(2,1)S(1)} %bitcast.7) | data formatting | bytes 2097152
  39.6 0.7 %copy.10 = bf16[1,128,512]{2,1,0:T(8,128)(2,1)} copy(bf16[1,128,512]{2,1,0:T(8,128)(2,1)S(1)} %bitcast.8) | data formatting | bytes 262144
Async XLA Ops:
  0.6 0.7 %copy-start.4 = (s32[1,2,2]{2,1,0:T(2,128)S(1)}, s32[1,2,2]{2,1,0:T(2,128)}, u32[]{:S(2)}) copy-start(s32[1,2,2]{2,1,0:T(2,128)} %param.9) | copy-start | bytes 52
  1.3 1.2 %copy-start = (bf16[1,128,4096]{2,1,0:T(8,128)(2,1)S(1)}, bf16[1,128,4096]{2,1,0:T(8,128)(2,1)}, u32[]{:S(2)}) copy-start(bf16[1,128,4096]{2,1,0:T(8,128)(2,1)} %param.5) | copy-start | bytes 3145732
  2.5 1.2 %copy-start.1 = (bf16[1,128,4096]{2,1,0:T(8,128)(2,1)S(1)}, bf16[1,128,4096]{2,1,0:T(8,128)(2,1)}, u32[]{:S(2)}) copy-start(bf16[1,128,4096]{2,1,0:T(8,128)(2,1)} %param.8) | copy-start | bytes 3145732
  3.8 0.9 %copy-start.2 = (bf16[1,128,512]{2,1,0:T(8,128)(2,1)S(1)}, bf16[1,128,512]{2,1,0:T(8,128)(2,1)}, u32[]{:S(2)}) copy-start(bf16[1,128,512]{2,1,0:T(8,128)(2,1)} %param.6) | copy-start | bytes 393220
  4.7 0.9 %copy-start.3 = (bf16[1,128,512]{2,1,0:T(8,128)(2,1)S(1)}, bf16[1,128,512]{2,1,0:T(8,128)(2,1)}, u32[]{:S(2)}) copy-start(bf16[1,128,512]{2,1,0:T(8,128)(2,1)} %param.7) | copy-start | bytes 393220

commit v2 on v1

--- a/solution.py
+++ b/solution.py
@@ -16,14 +16,16 @@
 REACH = 2
 MESH = pl.DeviceIdType.MESH
 NEG = -1e30
-
-
-def stacked(ref, block, group):
+PIECES = [(g, b, 0, SHARE) for g in range(GROUPS) for b in range(BLOCKS)][:-1]
+PIECES += [(GROUPS - 1, BLOCKS - 1, 0, 4), (GROUPS - 1, BLOCKS - 1, 4, 2), (GROUPS - 1, BLOCKS - 1, 6, 2)]
+
+
+def stacked(ref, block, group, first=0, heads=SHARE):
     rows = pl.ds(block * BLOCK, BLOCK)
     return jnp.concatenate(
         [
             ref[rows, pl.ds(pl.multiple_of(group * SHARE * SIZE, SIZE) + h * SIZE, SIZE)]
-            for h in range(SHARE)
+            for h in range(first, first + heads)
         ],
         axis=0,
     )
@@ -38,8 +40,8 @@
 
 
 def kernel(
-    pipes, ranks, entries, q_hbm, k_hbm, v_hbm, g_hbm, dq_hbm, dk_hbm,
-    qbuf, gbuf, kwin, vwin, kpar, vpar, prob, dqbuf, own, msg, arrived, dkbuf,
+    pipes, ranks, e_hbm, q_hbm, k_hbm, v_hbm, g_hbm, dq_hbm, dk_hbm,
+    entries, qbuf, gbuf, kwin, vwin, kpar, vpar, prob, dqbuf, own, msg, arrived, dkbuf,
     load_sem, halo_send, halo_recv, grad_send, grad_recv, msg_send, msg_recv, out_sem,
 ):
     pipe = lax.axis_index("pipe")
@@ -64,6 +66,7 @@
         pltpu.make_async_copy(q_hbm, qbuf, load_sem.at[0]),
         pltpu.make_async_copy(k_hbm, kwin.at[last], load_sem.at[1]),
         pltpu.make_async_copy(v_hbm, vwin.at[last], load_sem.at[2]),
+        pltpu.make_async_copy(e_hbm, entries, load_sem.at[3]),
     ]
     for load in loads:
         load.start()
@@ -84,14 +87,17 @@
                 )
             )
 
-    def grad_copy(group, block):
-        part = pl.ds(block * BLOCK, BLOCK)
-        lanes = pl.ds(group * SHARE * SIZE, SHARE * SIZE)
+    def place_of(piece):
+        group, block, first, heads = piece
+        return pl.ds(block * BLOCK, BLOCK), pl.ds((group * SHARE + first) * SIZE, heads * SIZE)
+
+    def grad_copy(index):
+        part, lanes = place_of(PIECES[index])
         return pltpu.make_async_remote_copy(
             src_ref=g_hbm.at[part, lanes],
             dst_ref=gbuf.at[part, lanes],
-            send_sem=grad_send.at[group, block],
-            recv_sem=grad_recv.at[group, block],
+            send_sem=grad_send.at[index],
+            recv_sem=grad_recv.at[index],
             device_id=pipe_at(-1),
             device_id_type=MESH,
         )
@@ -106,14 +112,12 @@
             device_id_type=MESH,
         )
 
-    grads = [[grad_copy(group, block) for block in range(BLOCKS)] for group in range(GROUPS)]
-    grads[0][0].start()
+    grads = [grad_copy(index) for index in range(len(PIECES))]
+    grads[0].start()
     for halo in halos:
         halo.start()
-    for group in range(GROUPS):
-        for block in range(BLOCKS):
-            if (group, block) != (0, 0):
-                grads[group][block].start()
+    for grad in grads[1:]:
+        grad.start()
     for load in loads:
         load.wait()
     for halo in halos:
@@ -160,81 +164,90 @@
 
     lax.fori_loop(0, GROUPS, forward, 0)
 
-    def backward(group, block):
-        soft = prob[group, block]
-        dprob = nt(chosen(vwin, vpar, group, block), stacked(gbuf, block, group))
+    def backward(piece):
+        group, block, first, heads = piece
+        soft = prob[group, block, :, pl.ds(first * BLOCK, heads * BLOCK)]
+        dprob = nt(chosen(vwin, vpar, group, block), stacked(gbuf, block, group, first, heads))
         dot = jnp.sum(soft * dprob, axis=0, keepdims=True)
         dscore = (soft * (dprob - dot)).astype(jnp.bfloat16)
-        dkey = (
-            jnp.dot(dscore, stacked(qbuf, block, group), preferred_element_type=jnp.float32) * scale
-        )
-        return dscore, dkey
-
-    def query_part(group, block, dscore):
+        queries = stacked(qbuf, block, group, first, heads)
+        return dscore, jnp.dot(dscore, queries, preferred_element_type=jnp.float32) * scale
+
+    def query_part(piece, dscore):
+        group, block, first, heads = piece
         dquery = (tn(dscore, chosen(kwin, kpar, group, block)) * scale).astype(jnp.bfloat16)
-        for h in range(SHARE):
-            dqbuf[pl.ds(block * BLOCK, BLOCK), pl.ds((group * SHARE + h) * SIZE, SIZE)] = dquery[
-                h * BLOCK : (h + 1) * BLOCK
-            ]
+        for h in range(heads):
+            dqbuf[pl.ds(block * BLOCK, BLOCK), pl.ds((group * SHARE + first + h) * SIZE, SIZE)] = (
+                dquery[h * BLOCK : (h + 1) * BLOCK]
+            )
 
     writes = []
 
-    def write_query(group, block):
-        part = pl.ds(block * BLOCK, BLOCK)
-        lanes = pl.ds(group * SHARE * SIZE, SHARE * SIZE)
+    def write_query(index):
+        part, lanes = place_of(PIECES[index])
         write = pltpu.make_async_copy(
-            dqbuf.at[part, lanes], dq_hbm.at[part, lanes], out_sem.at[group * BLOCKS + block]
+            dqbuf.at[part, lanes], dq_hbm.at[part, lanes], out_sem.at[index]
         )
         write.start()
         writes.append(write)
 
-    for group in range(GROUPS):
-        grads[group][0].wait_recv()
-        dscore0, dkey0 = backward(group, 0)
-        query_part(group, 0, dscore0)
-        write_query(group, 0)
-        grads[group][1].wait_recv()
-        dscore1, dkey1 = backward(group, 1)
-        parent0, parent1 = dkey0[BLOCK:], dkey1[BLOCK:]
-
-        def at_slot(slot):
-            total = jnp.zeros((BLOCK, SIZE), jnp.float32)
-            for block, parent in enumerate((parent0, parent1)):
-                if block <= slot < REACH * BLOCKS + block:
-                    total = total + jnp.where(slots[block] == slot, parent, 0.0)
-            return total
-
-        for reach in (2, 1):
-            first = (REACH - reach) * BLOCKS
-            for block in range(BLOCKS):
-                msg[reach - 1, group, pl.ds(block * BLOCK, BLOCK)] = at_slot(first + block).astype(
-                    jnp.bfloat16
-                )
-            msg_copy(group, reach).start()
-        own[group, :BLOCK] = dkey0[:BLOCK] + at_slot(REACH * BLOCKS)
-        own[group, BLOCK:] = dkey1[:BLOCK]
-        query_part(group, 1, dscore1)
-        write_query(group, 1)
-
+    totals = {}
+    for index, piece in enumerate(PIECES):
+        group, block = piece[:2]
+        grads[index].wait_recv()
+        dscore, dkey = backward(piece)
+        totals[group, block] = totals[group, block] + dkey if (group, block) in totals else dkey
+        if index + 1 == len(PIECES) or PIECES[index + 1][0] != group:
+            parents = [totals[group, other][BLOCK:] for other in range(BLOCKS)]
+
+            def at_slot(slot):
+                total = jnp.zeros((BLOCK, SIZE), jnp.float32)
+                for other, parent in enumerate(parents):
+                    if other <= slot < REACH * BLOCKS + other:
+                        total = total + jnp.where(slots[other] == slot, parent, 0.0)
+                return total
+
+            for reach in (2, 1):
+                begin = (REACH - reach) * BLOCKS
+                for other in range(BLOCKS):
+                    msg[reach - 1, group, pl.ds(other * BLOCK, BLOCK)] = at_slot(
+                        begin + other
+                    ).astype(jnp.bfloat16)
+                msg_copy(group, reach).start()
+            own[group, :BLOCK] = totals[group, 0][:BLOCK] + at_slot(REACH * BLOCKS)
+            own[group, BLOCK:] = totals[group, 1][:BLOCK]
+        query_part(piece, dscore)
+        write_query(index)
+
+    for halo in halos:
+        halo.wait_send()
+    for grad in grads:
+        grad.wait_send()
     for group in range(GROUPS):
         total = own[group]
         for reach in (1, 2):
             msg_copy(group, reach).wait_recv()
             total = total + arrived[reach - 1, group].astype(jnp.float32)
         dkbuf[:, pl.ds(group * SIZE, SIZE)] = total.astype(jnp.bfloat16)
-    write = pltpu.make_async_copy(dkbuf, dk_hbm, out_sem.at[GROUPS * BLOCKS])
+    write = pltpu.make_async_copy(dkbuf, dk_hbm, out_sem.at[len(PIECES)])
     write.start()
     writes.append(write)
-
-    for halo in halos:
-        halo.wait_send()
     for group in range(GROUPS):
-        for block in range(BLOCKS):
-            grads[group][block].wait_send()
         for reach in (1, 2):
             msg_copy(group, reach).wait_send()
     for write in writes:
         write.wait()
+
+
+def finish(dq_in, dk_in, dq_out, dk_out, sem):
+    copies = [
+        pltpu.make_async_copy(dq_in, dq_out, sem.at[0]),
+        pltpu.make_async_copy(dk_in, dk_out, sem.at[1]),
+    ]
+    for copy in copies:
+        copy.start()
+    for copy in copies:
+        copy.wait()
 
 
 def solution(mesh):
@@ -251,9 +264,10 @@
                 jax.ShapeDtypeStruct((rows, wide), jnp.bfloat16),
                 jax.ShapeDtypeStruct((rows, narrow), jnp.bfloat16),
             ),
-            in_specs=[pl.BlockSpec(memory_space=pltpu.SMEM)] + [anywhere] * 4,
+            in_specs=[pl.BlockSpec(memory_space=pltpu.HBM)] * 5,
             out_specs=(anywhere, anywhere),
             scratch_shapes=[
+                pltpu.SMEM((BLOCKS, 2), jnp.int32),
                 pltpu.VMEM((rows, wide), jnp.bfloat16),
                 pltpu.VMEM((rows, wide), jnp.bfloat16),
                 pltpu.VMEM(((REACH + 1) * rows, narrow), jnp.bfloat16),
@@ -266,14 +280,14 @@
                 pltpu.VMEM((REACH, GROUPS, rows, SIZE), jnp.bfloat16),
                 pltpu.VMEM((REACH, GROUPS, rows, SIZE), jnp.bfloat16),
                 pltpu.VMEM((rows, narrow), jnp.bfloat16),
-                dma((3,)),
+                dma((4,)),
                 dma((REACH, 2)),
                 dma((REACH, 2)),
-                dma((GROUPS, BLOCKS)),
-                dma((GROUPS, BLOCKS)),
+                dma((len(PIECES),)),
+                dma((len(PIECES),)),
                 dma((REACH, GROUPS)),
                 dma((REACH, GROUPS)),
-                dma((GROUPS * BLOCKS + 1,)),
+                dma((len(PIECES) + 1,)),
             ],
             compiler_params=pltpu.CompilerParams(
                 collective_id=0, has_side_effects=True, vmem_limit_bytes=32 * 1024 * 1024
@@ -281,7 +295,18 @@
             cost_estimate=pl.CostEstimate(
                 flops=700_000_000, bytes_accessed=4_000_000, transcendentals=600_000
             ),
-        )(key_blocks[0], query[0], key[0], value[0], grad[0])
+        )(*[pltpu.with_memory_space_constraint(x[0], pltpu.HBM) for x in (key_blocks, query, key, value, grad)])
+        dq, dk = pl.pallas_call(
+            finish,
+            out_shape=(
+                jax.ShapeDtypeStruct((rows, wide), jnp.bfloat16),
+                jax.ShapeDtypeStruct((rows, narrow), jnp.bfloat16),
+            ),
+            in_specs=[anywhere] * 2,
+            out_specs=[pl.BlockSpec(memory_space=pltpu.HBM)] * 2,
+            scratch_shapes=[dma((2,))],
+            compiler_params=pltpu.CompilerParams(vmem_limit_bytes=4 * 1024 * 1024),
+        )(*[pltpu.with_memory_space_constraint(x, pltpu.VMEM) for x in (dq, dk)])
         return dq[None], dk[None]
 
     spec = P("pipe", "ctx", None)

time: 40.5 us -> 34.5 us (0.85)
  local copies, waits for them, and re-layouts: 6.56 us -> 0 us
  Pallas kernels: 33 us -> 33.7 us
    unnamed x12 -> x0, local copies, waits for them, and re-layouts: 6.56 us -> none
    pallas_call x0 -> x1, Pallas kernels: none -> 1.02 us  [per_device(): pl.pallas_call(finish, out_shape=(jax.ShapeDtypeStruct((rows, wide), jnp....]
where the time goes in v2:
time: 34.5 us; the launch traced here: 34.3 us
  Pallas kernels  33.7 us (98%)
  between operations  0.64 us (2%)
    pallas_call x1, Pallas kernels, per_device(): pl.pallas_call(functools.partial(kernel, pipes, ranks), out_shape=(jax.Sh...  32.7 us
    pallas_call x1, Pallas kernels, per_device(): pl.pallas_call(finish, out_shape=(jax.ShapeDtypeStruct((rows, wide), jnp....  1.02 us

profile of v2, /device:TPU:0, one launch (start us, length us, event | category | flops | bytes accessed | tf_op | source)
XLA Modules:
  0.0 34.3 jit_solution(3530430221521883201)
XLA Ops:
  0.6 32.7 %shard_map.68 = (bf16[128,4096]{1,0:T(8,128)(2,1)S(1)}, bf16[128,512]{1,0:T(8,128)(2,1)S(1)}) custom-call(s32[2,2]{1,0:T(2,128)} %bitcast.13, bf16[128,4096]{1,0:T(8,128)(2,1)} %bitcast.7, bf16[128,512]{1,0:T(8,128)(2,1)} %bitcast.10, bf16[128,512]{1,0:T(8,128)(2,1)} %bitcast.11, bf16[128,4096]{1,0:T(8,128)(2,1)} %bitcast.8), custom_call_target="tpu_custom_call" | custom-call | flops 700000000 | bytes 4000000 | tf_op jit(solution)/shard_map/pallas_call | solution.py:261
  33.3 1.0 %shard_map.69 = (bf16[128,4096]{1,0:T(8,128)(2,1)}, bf16[128,512]{1,0:T(8,128)(2,1)}) custom-call(bf16[128,4096]{1,0:T(8,128)(2,1)S(1)} %get-tuple-element.6.dq_in, bf16[128,512]{1,0:T(8,128)(2,1)S(1)} %get-tuple-element.7.dk_in), custom_call_target="tpu_custom_call" | custom-call | tf_op jit(solution)/shard_map/pallas_call | solution.py:299

commit v3 on v2

--- a/solution.py
+++ b/solution.py
@@ -16,6 +16,7 @@
 REACH = 2
 MESH = pl.DeviceIdType.MESH
 NEG = -1e30
+CUTS = 1
 PIECES = [(g, b, 0, SHARE) for g in range(GROUPS) for b in range(BLOCKS)][:-1]
 PIECES += [(GROUPS - 1, BLOCKS - 1, 0, 4), (GROUPS - 1, BLOCKS - 1, 4, 2), (GROUPS - 1, BLOCKS - 1, 6, 2)]
 
@@ -40,9 +41,9 @@
 
 
 def kernel(
-    pipes, ranks, e_hbm, q_hbm, k_hbm, v_hbm, g_hbm, dq_hbm, dk_hbm,
-    entries, qbuf, gbuf, kwin, vwin, kpar, vpar, prob, dqbuf, own, msg, arrived, dkbuf,
-    load_sem, halo_send, halo_recv, grad_send, grad_recv, msg_send, msg_recv, out_sem,
+    pipes, ranks, e_hbm, q_hbm, k_hbm, v_hbm, g_hbm, dq_ref, dk_ref,
+    entries, qbuf, gbuf, kwin, vwin, kpar, vpar, prob, own, msg, arrived, note, notes,
+    load_sem, halo_send, halo_recv, grad_send, grad_recv, msg_send, msg_recv, note_send, note_recv,
 ):
     pipe = lax.axis_index("pipe")
     rank = lax.axis_index("ctx")
@@ -102,15 +103,27 @@
             device_id_type=MESH,
         )
 
-    def msg_copy(group, reach):
+    def msg_copy(group, block, reach):
         return pltpu.make_async_remote_copy(
-            src_ref=msg.at[reach - 1, group],
-            dst_ref=arrived.at[reach - 1, group],
-            send_sem=msg_send.at[reach - 1, group],
-            recv_sem=msg_recv.at[reach - 1, group],
+            src_ref=msg.at[group, block],
+            dst_ref=arrived.at[reach - 1, group, block],
+            send_sem=msg_send.at[reach - 1, group, block],
+            recv_sem=msg_recv.at[reach - 1, group, block],
             device_id=ctx_at(-reach),
             device_id_type=MESH,
         )
+
+    note_copies = [
+        pltpu.make_async_remote_copy(
+            src_ref=note,
+            dst_ref=notes.at[reach - 1],
+            send_sem=note_send.at[reach - 1],
+            recv_sem=note_recv.at[reach - 1],
+            device_id=ctx_at(-reach),
+            device_id_type=MESH,
+        )
+        for reach in (1, 2)
+    ]
 
     grads = [grad_copy(index) for index in range(len(PIECES))]
     grads[0].start()
@@ -126,6 +139,11 @@
     def slot_of(block, shape):
         entry = jnp.full(shape, entries[block, 1], jnp.int32)
         return jnp.where(entry >= 0, entry - (rank - REACH) * BLOCKS, -1)
+
+    for block in range(BLOCKS):
+        note[block] = slot_of(block, (8, SIZE))
+    for copy in note_copies:
+        copy.start()
 
     for block in range(BLOCKS):
         wide = slot_of(block, (BLOCK, narrow))
@@ -177,73 +195,69 @@
         group, block, first, heads = piece
         dquery = (tn(dscore, chosen(kwin, kpar, group, block)) * scale).astype(jnp.bfloat16)
         for h in range(heads):
-            dqbuf[pl.ds(block * BLOCK, BLOCK), pl.ds((group * SHARE + first + h) * SIZE, SIZE)] = (
+            dq_ref[pl.ds(block * BLOCK, BLOCK), pl.ds((group * SHARE + first + h) * SIZE, SIZE)] = (
                 dquery[h * BLOCK : (h + 1) * BLOCK]
             )
 
-    writes = []
-
-    def write_query(index):
-        part, lanes = place_of(PIECES[index])
-        write = pltpu.make_async_copy(
-            dqbuf.at[part, lanes], dq_hbm.at[part, lanes], out_sem.at[index]
-        )
-        write.start()
-        writes.append(write)
+    def close(group):
+        parts = [own[group, :BLOCK], own[group, BLOCK:]]
+        for reach in range(1, REACH + 1):
+            for sent in range(BLOCKS):
+                msg_copy(group, sent, reach).wait_recv()
+                slot = jnp.broadcast_to(notes[reach - 1, sent, :1], (BLOCK, SIZE))
+                part = arrived[reach - 1, group, sent].astype(jnp.float32)
+                for mine in range(BLOCKS):
+                    hit = slot == (REACH - reach) * BLOCKS + mine
+                    parts[mine] = parts[mine] + jnp.where(hit, part, 0.0)
+        for mine in range(BLOCKS):
+            dk_ref[pl.ds(mine * BLOCK, BLOCK), pl.ds(group * SIZE, SIZE)] = parts[mine].astype(
+                jnp.bfloat16
+            )
 
     totals = {}
     for index, piece in enumerate(PIECES):
         group, block = piece[:2]
         grads[index].wait_recv()
         dscore, dkey = backward(piece)
-        totals[group, block] = totals[group, block] + dkey if (group, block) in totals else dkey
-        if index + 1 == len(PIECES) or PIECES[index + 1][0] != group:
-            parents = [totals[group, other][BLOCK:] for other in range(BLOCKS)]
-
-            def at_slot(slot):
-                total = jnp.zeros((BLOCK, SIZE), jnp.float32)
-                for other, parent in enumerate(parents):
-                    if other <= slot < REACH * BLOCKS + other:
-                        total = total + jnp.where(slots[other] == slot, parent, 0.0)
-                return total
-
+        totals[block] = totals[block] + dkey if piece[2] else dkey
+        if piece[2] + piece[3] == SHARE:
+            parent = totals[block][BLOCK:]
+            msg[group, block] = parent.astype(jnp.bfloat16)
             for reach in (2, 1):
-                begin = (REACH - reach) * BLOCKS
-                for other in range(BLOCKS):
-                    msg[reach - 1, group, pl.ds(other * BLOCK, BLOCK)] = at_slot(
-                        begin + other
-                    ).astype(jnp.bfloat16)
-                msg_copy(group, reach).start()
-            own[group, :BLOCK] = totals[group, 0][:BLOCK] + at_slot(REACH * BLOCKS)
-            own[group, BLOCK:] = totals[group, 1][:BLOCK]
+                msg_copy(group, block, reach).start()
+            own[group, pl.ds(block * BLOCK, BLOCK)] = totals[block][:BLOCK]
+            if block:
+                near = jnp.where(slots[block] == REACH * BLOCKS, parent, 0.0)
+                own[group, :BLOCK] = own[group, :BLOCK] + near
         query_part(piece, dscore)
-        write_query(index)
+        if index + 3 == len(PIECES):
+            for copy in note_copies:
+                copy.wait_recv()
+            for earlier in range(GROUPS - 1):
+                close(earlier)
 
     for halo in halos:
         halo.wait_send()
+    for copy in note_copies:
+        copy.wait_send()
     for grad in grads:
         grad.wait_send()
-    for group in range(GROUPS):
-        total = own[group]
+    for group in range(GROUPS - 1):
+        for sent in range(BLOCKS):
+            for reach in (1, 2):
+                msg_copy(group, sent, reach).wait_send()
+    close(GROUPS - 1)
+    for sent in range(BLOCKS):
         for reach in (1, 2):
-            msg_copy(group, reach).wait_recv()
-            total = total + arrived[reach - 1, group].astype(jnp.float32)
-        dkbuf[:, pl.ds(group * SIZE, SIZE)] = total.astype(jnp.bfloat16)
-    write = pltpu.make_async_copy(dkbuf, dk_hbm, out_sem.at[len(PIECES)])
-    write.start()
-    writes.append(write)
-    for group in range(GROUPS):
-        for reach in (1, 2):
-            msg_copy(group, reach).wait_send()
-    for write in writes:
-        write.wait()
+            msg_copy(GROUPS - 1, sent, reach).wait_send()
 
 
 def finish(dq_in, dk_in, dq_out, dk_out, sem):
-    copies = [
-        pltpu.make_async_copy(dq_in, dq_out, sem.at[0]),
-        pltpu.make_async_copy(dk_in, dk_out, sem.at[1]),
-    ]
+    rows = dq_in.shape[0] // CUTS
+    copies = [pltpu.make_async_copy(dk_in, dk_out, sem.at[CUTS])]
+    for cut in range(CUTS):
+        part = pl.ds(cut * rows, rows)
+        copies.append(pltpu.make_async_copy(dq_in.at[part], dq_out.at[part], sem.at[cut]))
     for copy in copies:
         copy.start()
     for copy in copies:
@@ -265,7 +279,7 @@
                 jax.ShapeDtypeStruct((rows, narrow), jnp.bfloat16),
             ),
             in_specs=[pl.BlockSpec(memory_space=pltpu.HBM)] * 5,
-            out_specs=(anywhere, anywhere),
+            out_specs=(pl.BlockSpec(memory_space=pltpu.VMEM),) * 2,
             scratch_shapes=[
                 pltpu.SMEM((BLOCKS, 2), jnp.int32),
                 pltpu.VMEM((rows, wide), jnp.bfloat16),
@@ -275,19 +289,20 @@
                 pltpu.VMEM((BLOCKS, BLOCK, narrow), jnp.bfloat16),
                 pltpu.VMEM((BLOCKS, BLOCK, narrow), jnp.bfloat16),
                 pltpu.VMEM((GROUPS, BLOCKS, 2 * BLOCK, SHARE * BLOCK), jnp.float32),
-                pltpu.VMEM((rows, wide), jnp.bfloat16),
                 pltpu.VMEM((GROUPS, rows, SIZE), jnp.float32),
-                pltpu.VMEM((REACH, GROUPS, rows, SIZE), jnp.bfloat16),
-                pltpu.VMEM((REACH, GROUPS, rows, SIZE), jnp.bfloat16),
-                pltpu.VMEM((rows, narrow), jnp.bfloat16),
+                pltpu.VMEM((GROUPS, BLOCKS, BLOCK, SIZE), jnp.bfloat16),
+                pltpu.VMEM((REACH, GROUPS, BLOCKS, BLOCK, SIZE), jnp.bfloat16),
+                pltpu.VMEM((BLOCKS, 8, SIZE), jnp.int32),
+                pltpu.VMEM((REACH, BLOCKS, 8, SIZE), jnp.int32),
                 dma((4,)),
                 dma((REACH, 2)),
                 dma((REACH, 2)),
                 dma((len(PIECES),)),
                 dma((len(PIECES),)),
-                dma((REACH, GROUPS)),
-                dma((REACH, GROUPS)),
-                dma((len(PIECES) + 1,)),
+                dma((REACH, GROUPS, BLOCKS)),
+                dma((REACH, GROUPS, BLOCKS)),
+                dma((REACH,)),
+                dma((REACH,)),
             ],
             compiler_params=pltpu.CompilerParams(
                 collective_id=0, has_side_effects=True, vmem_limit_bytes=32 * 1024 * 1024
@@ -304,7 +319,7 @@
             ),
             in_specs=[anywhere] * 2,
             out_specs=[pl.BlockSpec(memory_space=pltpu.HBM)] * 2,
-            scratch_shapes=[dma((2,))],
+            scratch_shapes=[dma((CUTS + 1,))],
             compiler_params=pltpu.CompilerParams(vmem_limit_bytes=4 * 1024 * 1024),
         )(*[pltpu.with_memory_space_constraint(x, pltpu.VMEM) for x in (dq, dk)])
         return dq[None], dk[None]

time: 34.5 us -> 34.2 us (level)
  no operation moved by 1% of the time
where the time goes in v3:
time: 34.2 us; the launch traced here: 34.1 us
  Pallas kernels  33.4 us (98%)
  between operations  0.64 us (2%)
    pallas_call x1, Pallas kernels, per_device(): pl.pallas_call(functools.partial(kernel, pipes, ranks), out_shape=(jax.Sh...  32.4 us
    pallas_call x1, Pallas kernels, per_device(): pl.pallas_call(finish, out_shape=(jax.ShapeDtypeStruct((rows, wide), jnp....  1.03 us

profile of v3, /device:TPU:0, one launch (start us, length us, event | category | flops | bytes accessed | tf_op | source)
XLA Modules:
  0.0 34.1 jit_solution(1151424583461923220)
XLA Ops:
  0.6 32.4 %shard_map.68 = (bf16[128,4096]{1,0:T(8,128)(2,1)S(1)}, bf16[128,512]{1,0:T(8,128)(2,1)S(1)}) custom-call(s32[2,2]{1,0:T(2,128)} %bitcast.13, bf16[128,4096]{1,0:T(8,128)(2,1)} %bitcast.7, bf16[128,512]{1,0:T(8,128)(2,1)} %bitcast.10, bf16[128,512]{1,0:T(8,128)(2,1)} %bitcast.11, bf16[128,4096]{1,0:T(8,128)(2,1)} %bitcast.8), custom_call_target="tpu_custom_call" | custom-call | flops 700000000 | bytes 4000000 | tf_op jit(solution)/shard_map/pallas_call | solution.py:275
  33.0 1.0 %shard_map.69 = (bf16[128,4096]{1,0:T(8,128)(2,1)}, bf16[128,512]{1,0:T(8,128)(2,1)}) custom-call(bf16[128,4096]{1,0:T(8,128)(2,1)S(1)} %get-tuple-element.6.dq_in, bf16[128,512]{1,0:T(8,128)(2,1)S(1)} %get-tuple-element.7.dk_in), custom_call_target="tpu_custom_call" | custom-call | tf_op jit(solution)/shard_map/pallas_call | solution.py:314

commit v4 on v3

--- a/solution.py
+++ b/solution.py
@@ -18,7 +18,7 @@
 NEG = -1e30
 CUTS = 1
 PIECES = [(g, b, 0, SHARE) for g in range(GROUPS) for b in range(BLOCKS)][:-1]
-PIECES += [(GROUPS - 1, BLOCKS - 1, 0, 4), (GROUPS - 1, BLOCKS - 1, 4, 2), (GROUPS - 1, BLOCKS - 1, 6, 2)]
+PIECES += [(GROUPS - 1, BLOCKS - 1, 0, 4), (GROUPS - 1, BLOCKS - 1, 4, 4)]
 
 
 def stacked(ref, block, group, first=0, heads=SHARE):
@@ -230,7 +230,7 @@
                 near = jnp.where(slots[block] == REACH * BLOCKS, parent, 0.0)
                 own[group, :BLOCK] = own[group, :BLOCK] + near
         query_part(piece, dscore)
-        if index + 3 == len(PIECES):
+        if index + 2 == len(PIECES):
             for copy in note_copies:
                 copy.wait_recv()
             for earlier in range(GROUPS - 1):

time: 34.2 us -> 34.2 us (level)
  no operation moved by 1% of the time
where the time goes in v4:
time: 34.2 us; the launch traced here: 34 us
  Pallas kernels  33.4 us (98%)
  between operations  0.64 us (2%)
    pallas_call x1, Pallas kernels, per_device(): pl.pallas_call(functools.partial(kernel, pipes, ranks), out_shape=(jax.Sh...  32.4 us
    pallas_call x1, Pallas kernels, per_device(): pl.pallas_call(finish, out_shape=(jax.ShapeDtypeStruct((rows, wide), jnp....  1.03 us

profile of v4, /device:TPU:0, one launch (start us, length us, event | category | flops | bytes accessed | tf_op | source)
XLA Modules:
  0.0 34.0 jit_solution(9078799844100271132)
XLA Ops:
  0.6 32.4 %shard_map.68 = (bf16[128,4096]{1,0:T(8,128)(2,1)S(1)}, bf16[128,512]{1,0:T(8,128)(2,1)S(1)}) custom-call(s32[2,2]{1,0:T(2,128)} %bitcast.13, bf16[128,4096]{1,0:T(8,128)(2,1)} %bitcast.7, bf16[128,512]{1,0:T(8,128)(2,1)} %bitcast.10, bf16[128,512]{1,0:T(8,128)(2,1)} %bitcast.11, bf16[128,4096]{1,0:T(8,128)(2,1)} %bitcast.8), custom_call_target="tpu_custom_call" | custom-call | flops 700000000 | bytes 4000000 | tf_op jit(solution)/shard_map/pallas_call | solution.py:275
  33.0 1.0 %shard_map.69 = (bf16[128,4096]{1,0:T(8,128)(2,1)}, bf16[128,512]{1,0:T(8,128)(2,1)}) custom-call(bf16[128,4096]{1,0:T(8,128)(2,1)S(1)} %get-tuple-element.6.dq_in, bf16[128,512]{1,0:T(8,128)(2,1)S(1)} %get-tuple-element.7.dk_in), custom_call_target="tpu_custom_call" | custom-call | tf_op jit(solution)/shard_map/pallas_call | solution.py:314
